TPU v7x, 128 devices: a whole 4x4x4 slice. The times are simulated.
128 devices in a mesh: dp: 8 (over x_hi, z), tensor: 16 (over x_lo, y, core).
Axes of the slice: x: 4 (x_hi: 2, x_lo: 2; x = x_hi * 2 + x_lo), y: 4, z: 4, core: 2. Of those that a mesh axis runs over, the one named last changes fastest.
Arguments:
- ckpt_values: bfloat16 [2048, 18432], P(('dp', 'tensor')), may hold values from -6 to 6
- ckpt_scales: bfloat16 [2048, 144], P(('dp', 'tensor')), may hold values from 0.25 to 4
- norm_gain: float32 [18432], replicated, may hold values from 0.5 to 1.5
- pre_act: bfloat16 [2048, 36864], P('dp', 'tensor'), may hold values from -6 to 6
- act_grad: bfloat16 [2048, 36864], P('dp', 'tensor'), may hold values from -0.09375 to 0.09375
Outputs:
- weight_grad: bfloat16 [18432, 36864], P('dp', 'tensor')
All inputs are finite; a program needn't handle non-finite values.
Results may differ from a plain program's by a relative error of at most 0.0057.
Values may be sent and summed in bfloat16 or wider, within the bound.
A program may use at most 128 MiB of HBM per device.

v0:
```python
import jax
import jax.numpy as jnp
from jax import lax
from jax.sharding import PartitionSpec as P

QB = 128


def normalize(values, scales, gain):
    count = values.shape[0]
    width = values.shape[1]
    inputs = (
        values.astype(jnp.float32).reshape(count, width // QB, QB)
        * scales.astype(jnp.float32)[:, :, None]
    )
    inputs = inputs.reshape(count, width)
    inverse = lax.rsqrt(jnp.mean(inputs * inputs, axis=1, keepdims=True) + 1e-05)
    return (inputs * inverse * gain).astype(jnp.bfloat16)


def on_device(ckpt_values, ckpt_scales, norm_gain, pre_act, act_grad):
    pre_grad = (
        act_grad.astype(jnp.float32) * 2.0 * jnp.maximum(pre_act.astype(jnp.float32), 0.0)
    ).astype(jnp.bfloat16)
    normed = normalize(ckpt_values, ckpt_scales, norm_gain)
    gathered = lax.all_gather(normed, "tensor", axis=0, tiled=True)
    grouped = lax.all_to_all(gathered[None], "dp", split_axis=2, concat_axis=0, tiled=True)
    features = grouped.reshape(grouped.shape[0] * grouped.shape[1], grouped.shape[2])
    total = lax.dot_general(
        features,
        lax.all_gather(pre_grad, "dp", axis=0, tiled=True),
        (((0,), (0,)), ((), ())),
        preferred_element_type=jnp.float32,
    )
    return total.astype(jnp.bfloat16)


def solution(mesh):
    in_specs = (
        P(("dp", "tensor"), None),
        P(("dp", "tensor"), None),
        P(),
        P("dp", "tensor"),
        P("dp", "tensor"),
    )
    out_specs = P("dp", "tensor")
    return jax.shard_map(
        on_device, mesh=mesh, in_specs=in_specs, out_specs=out_specs, check_vma=False
    )
```

profile of v0, /device:TPU:1, one launch (start us, length us, event | category | flops | bytes accessed | tf_op | source)
XLA Modules:
  0.0 404.2 jit_solution(7969495020714175538)
XLA Ops:
  6.5 0.0 copy-start
  6.5 0.0 copy-start.3
  6.5 0.0 all-gather.3.cloned.1.call-start
  6.5 1.1 mul.39
  7.7 0.0 copy-start.1
  7.7 0.0 copy-start.2
  7.7 1.7 multiply_reduce_fusion
  9.4 0.0 copy-done
  9.4 0.0 copy-done.3
  9.4 1.3 multiply_convert_fusion.1
  10.7 0.0 all-gather.3.cloned.1.call-update
  10.7 0.0 all-gather.5.cloned.1.call-start
  10.7 0.0 copy-done.1
  10.8 0.0 copy-done.2
  10.8 1.5 multiply_convert_fusion
  12.2 0.0 all-gather.5.cloned.1.call-update
  12.2 59.3 %all-gather.3.cloned.1.call-done = bf16[256,18432]{1,0:T(8,128)(2,1)} async-done(((bf16[16,18432]{1,0:T(8,128)(2,1)}), bf16[256,18432]{1,0:T(8,128)(2,1)}) %all-gather.3.cloned.1.call-update) | async-done | bytes 9437200 | tf_op jit(solution)/shard_map/all_gather | solution.py:26
  71.5 38.5 %copy.9 = bf16[1,256,18432]{1,0,2:T(2,128)(2,1)} copy(bf16[1,256,18432]{2,1,0:T(8,128)(2,1)} %bitcast.21) | data formatting | bytes 18874368 | tf_op jit(solution)/shard_map/broadcast_in_dim | solution.py:27
  110.0 0.5 broadcast.24
  110.5 95.0 %reduce = bf16[18432,256]{1,0:T(8,128)(2,1)} reduce(bf16[18432,1,256]{2,1,0:T(2,128)(2,1)} %bitcast.17, bf16[]{:T(256)} %broadcast.24), dimensions={1}, to_apply=%bitcast.12.reduce_sub_computation | reduce | bytes 18874370
  205.6 10.4 %reshape.18 = bf16[8,2,294912]{2,1,0:T(2,128)(2,1)} reshape(bf16[18432,256]{1,0:T(8,128)(2,1)} %reduce) | data formatting | bytes 18874368
  215.9 112.3 %all_to_all.15 = bf16[8,2,294912]{2,1,0:T(2,128)(2,1)} all-to-all(bf16[8,2,294912]{2,1,0:T(2,128)(2,1)} %reshape.18), channel_id=1, replica_groups=mesh['dp'=8,'tensor'=16] {'dp'}, dimensions={0} | all-to-all | bytes 18874368 | tf_op jit(solution)/shard_map/all_to_all | solution.py:27
  328.3 14.5 %reshape.19 = bf16[18432,1,256]{2,1,0:T(2,128)(2,1)} reshape(bf16[8,2,294912]{2,1,0:T(2,128)(2,1)} %all_to_all.15) | data formatting | bytes 18874368
  342.7 12.7 %copy.11 = bf16[1,256,18432]{1,2,0:T(8,128)(2,1)} copy(bf16[1,256,18432]{1,0,2:T(2,128)(2,1)} %bitcast.16) | data formatting | bytes 18874368
  355.5 12.6 %copy.10 = bf16[8,1,256,2304]{3,2,0,1:T(8,128)(2,1)} copy(bf16[8,1,256,2304]{2,3,0,1:T(8,128)(2,1)} %bitcast.18) | data formatting | bytes 18874368 | tf_op jit(solution)/shard_map/all_to_all | solution.py:27
  368.1 0.0 all-gather.5.cloned.1.call-done
  368.1 29.3 %convolution_convert_fusion = bf16[2304,2304]{1,0:T(8,128)(2,1)} fusion(bf16[2048,2304]{1,0:T(8,128)(2,1)} %bitcast.22, bf16[2048,2304]{1,0:T(8,128)(2,1)} %all-gather.5.cloned.1.call-done), kind=kOutput, calls=%fused_computation | convolution fusion | flops 21748580352 | bytes 29491200 | tf_op jit(solution)/shard_map/dot_general | solution.py:29
  (1 shorter events, 0.0 us)
Async XLA Ops:
  6.5 2.9 copy-start
  6.5 2.9 copy-start.3
  6.5 65.0 %all-gather.3.cloned.1.call-start = ((), (), s32[]{:S(2)}) async-start(), calls=%async_computation.1 | async-start | bytes 10027008 | tf_op jit(solution)/shard_map/all_gather | solution.py:26
  7.7 3.1 copy-start.1
  7.7 3.1 copy-start.2
  10.7 357.4 %all-gather.5.cloned.1.call-start = ((), (), s32[]{:S(2)}) async-start(), calls=%async_computation.2 | async-start | bytes 10616832 | tf_op jit(solution)/shard_map/all_gather | solution.py:31
Sparse Core Ops, SparseCore 0:
  10.8 60.6 all-gather.2
  73.8 116.8 all-gather.4
where the time goes:
time: 407 us; the launch traced here: 404 us
  blocking collectives  112 us (28%)
  other arithmetic  99.5 us (24%)
  local copies, waits for them, and re-layouts  90.3 us (22%)
  waiting for transfers between devices  59.3 us (15%)
  matrix products  29.3 us (7%)
  between operations  13.5 us (3%)
    all_to_all x1, blocking collectives, on_device(): lax.all_to_all(gathered[None], 'dp', split_axis=2, concat_axis=0, tiled=T...  112 us
    unnamed x1, other arithmetic  95 us
    all_gather x1, waiting for transfers between devices, on_device(): gathered = lax.all_gather(normed, 'tensor', axis=0, tiled=True)  59.3 us
    broadcast_in_dim x1, local copies, waits for them, and re-layouts, on_device(): gathered[None]  38.5 us
    unnamed x12, local copies, waits for them, and re-layouts  38.1 us
    dot_general x1, matrix products, on_device(): lax.dot_general(features, lax.all_gather(pre_grad, 'dp', axis=0, tiled=Tr...  29.3 us
    all_to_all x1, local copies, waits for them, and re-layouts, on_device(): lax.all_to_all(gathered[None], 'dp', split_axis=2, concat_axis=0, tiled=T...  12.6 us
  transfers between devices with their start and end apart: 2, of which 1 were waited for; matrix products, arithmetic and copies ran while one was open for 46% of the time, Pallas kernels for 0%

commit v1 on v0

v1 whole, which is shorter than its diff:
```python
import functools

import jax
import jax.numpy as jnp
from jax import lax
from jax.experimental import pallas as pl
from jax.experimental.pallas import tpu as pltpu
from jax.sharding import PartitionSpec as P

MESH = pl.DeviceIdType.MESH
QB = 128
REPLICAS = 8
GROUP = 16
ROWS = 16
FEATURES = 2304
COLUMNS = 2304
WIDTH = 18432
HALF = 128
CHUNK = 64
MB = 768

SLOT = {(0, 0): 0, (0, -1): 1, (0, 1): 2, (1, 0): 3, (0, 2): 4, (1, -1): 5, (1, 1): 6, (1, 2): 7}
FAR = ((0, -1), (0, 1), (1, 0), (0, 2), (1, -1), (1, 1), (1, 2))
CONTRACT_FIRST = (((0,), (0,)), ((), ()))
COPIES = 64


def gather_kernel(
    values_hbm, scales_hbm, gain_hbm, pre_hbm, act_hbm,
    total, last_normed, last_grads,
    normed, grads, values, scales, gain, pre, act, scaled, own, send_sems, recv_sems, local_sems,
):
    dp, tensor = lax.axis_index("dp"), lax.axis_index("tensor")
    h, z = dp // 4, dp % 4
    xl, y, core = tensor // 8, (tensor // 2) % 4, tensor % 2

    def replica(dh, dz):
        return (h + dh) % 2 * 4 + (z + dz + 4) % 4

    def member(dx, dy, dc):
        return (xl + dx) % 2 * 8 + (y + dy + 4) % 4 * 2 + (core + dc) % 2

    def peer(dh=0, dz=0, dx=0, dy=0, dc=0):
        return replica(dh, dz), member(dx, dy, dc)

    started = []

    def send(src, dst, device):
        at = len(started)
        copy = pltpu.make_async_remote_copy(
            src_ref=src, dst_ref=dst, send_sem=send_sems.at[at], recv_sem=recv_sems.at[at],
            device_id=device, device_id_type=MESH,
        )
        copy.start()
        started.append(copy)
        return copy

    def load(src, dst, at):
        copy = pltpu.make_async_copy(src, dst, local_sems.at[at])
        copy.start()
        return copy

    def chunk(ref, c):
        return ref.at[c // 2, pl.ds(c % 2 * CHUNK, CHUNK)]

    pieces = {}
    for c in (0, 2):
        rows = pl.ds(c * CHUNK, CHUNK)
        pieces[c] = (load(pre_hbm.at[rows], pre.at[rows], 2 * c), load(act_hbm.at[rows], act.at[rows], 2 * c + 1))
    tokens = (load(values_hbm, values, 8), load(scales_hbm, scales, 9), load(gain_hbm, gain, 10))
    for c in (1, 3):
        rows = pl.ds(c * CHUNK, CHUNK)
        pieces[c] = (load(pre_hbm.at[rows], pre.at[rows], 2 * c), load(act_hbm.at[rows], act.at[rows], 2 * c + 1))

    friends = [peer(dh, dz) for dh, dz in FAR]
    friends += [peer(dx=1), peer(dy=1), peer(dy=-1), peer(dc=1)]
    barrier = pltpu.get_barrier_semaphore()
    for friend in friends:
        pl.semaphore_signal(barrier, inc=1, device_id=friend, device_id_type=MESH)

    def make_grad(c):
        for piece in pieces[c]:
            piece.wait()
        rows = pl.ds(c * CHUNK, CHUNK)
        product = act[rows].astype(jnp.float32) * 2.0 * jnp.maximum(pre[rows].astype(jnp.float32), 0.0)
        grads[0, c // 2, c % 2 * CHUNK : (c % 2 + 1) * CHUNK] = product.astype(jnp.bfloat16)

    def grad_send(slot, c, to_slot, **where):
        to = last_grads if to_slot == 7 else grads.at[to_slot]
        return send(chunk(grads.at[slot], c), chunk(to, c), peer(**where))

    up, down, over = {}, {}, {}

    def send_up(c):
        up[c] = grad_send(0, c, 1, dz=1)

    def send_down(c):
        down[c] = grad_send(0, c, 2, dz=-1)

    def send_over(c):
        over[c] = grad_send(0, c, 3, dh=1)

    make_grad(0)
    pl.semaphore_wait(barrier, len(friends))
    send_up(0)
    send_over(0)
    make_grad(2)
    send_down(2)

    for copy in tokens:
        copy.wait()
    squares = jnp.zeros((ROWS, QB), jnp.float32)
    for b in range(WIDTH // QB):
        at = slice(b * QB, (b + 1) * QB)
        block = values[:, at].astype(jnp.float32) * scales[:, b : b + 1].astype(jnp.float32)
        scaled[:, at] = block
        squares = squares + block * block
    mean = jnp.sum(squares, axis=1, keepdims=True) * (1.0 / WIDTH)
    inverse = lax.rsqrt(mean + 1e-05)
    for d in range(REPLICAS):
        at = slice(d * FEATURES, (d + 1) * FEATURES)
        own[d] = (scaled[:, at] * inverse * gain[:, at]).astype(jnp.bfloat16)

    def tokens_of(dx, dy, dc=0, slots=slice(None)):
        at = pl.multiple_of((y + dy + 4) % 4 * 32 + (core + dc) % 2 * 16, 16)
        return normed.at[slots, (xl + dx) % 2, pl.ds(at, ROWS)]

    def pair_of(dy, slots=slice(None)):
        at = pl.multiple_of((y + dy + 4) % 4 * 32 + core * 16, 16)
        return normed.at[slots, :, pl.ds(at, ROWS)]

    kept = load(own.at[dp], tokens_of(0, 0).at[0], 11)
    spread = []
    for dh, dz in FAR:
        spread.append(send(own.at[replica(dh, dz)], tokens_of(0, 0).at[SLOT[(dh, dz if dz == 2 else -dz)]], peer(dh, dz)))

    make_grad(1)
    make_grad(3)
    send_up(1)
    send_down(3)
    send_over(2)
    send_up(2)
    send_down(0)
    send_up(3)
    send_down(1)

    kept.wait()
    for copy in spread:
        copy.wait_recv()

    def same(ref, **where):
        return send(ref, ref, peer(**where))

    mine = tokens_of(0, 0)
    cross = same(mine, dx=1)
    mine_up, mine_down = same(mine, dy=1), same(mine, dy=-1)
    swap = [same(mine, dc=1)]
    send_over(1)
    send_over(3)

    up[0].wait_recv()
    f2_up = [grad_send(1, 0, 4, dz=1)]
    x2 = [grad_send(1, 0, 5, dh=1)]
    down[2].wait_recv()
    f2_down = [grad_send(2, 2, 4, dz=-1)]
    x2 += [grad_send(2, 2, 6, dh=1)]
    up[1].wait_recv()
    f2_up += [grad_send(1, 1, 4, dz=1)]
    down[3].wait_recv()
    f2_down += [grad_send(2, 3, 4, dz=-1)]

    cross.wait_recv()
    theirs = tokens_of(1, 0)
    theirs_up, theirs_down = same(theirs, dy=1), same(theirs, dy=-1)
    swap += [same(theirs, dc=1)]

    over[0].wait_recv()
    f3 = [grad_send(3, 0, 6, dz=-1)]
    over[2].wait_recv()
    f3 += [grad_send(3, 2, 5, dz=1)]

    mine_up.wait_recv()
    low, high = slice(0, 4), slice(4, 8)
    at_low, at_high = tokens_of(0, -1, slots=low), tokens_of(0, 1, slots=high)
    n2 = [same(at_low, dy=1)]
    mine_down.wait_recv()
    n2 += [same(at_high, dy=-1)]

    over[1].wait_recv()
    f3 += [grad_send(3, 1, 5, dz=1), grad_send(3, 1, 6, dz=-1)]
    over[3].wait_recv()
    f3 += [grad_send(3, 3, 5, dz=1), grad_send(3, 3, 6, dz=-1)]

    def accumulate(left, right, first=False):
        def step(m, carry):
            out_rows = pl.ds(pl.multiple_of(m * MB, MB), MB)
            part = lax.dot_general(
                left(out_rows), right(), CONTRACT_FIRST, preferred_element_type=jnp.float32
            )
            if first:
                total[out_rows, :] = part
            else:
                total[out_rows, :] += part
            return carry

        lax.fori_loop(0, FEATURES // MB, step, 0)

    def near(dy, first=False):
        at = pl.ds(pl.multiple_of((y + dy + 4) % 4 * 32, 32), 32)
        accumulate(
            lambda rows: normed[0:4, :, at, rows].reshape(256, MB),
            lambda: grads[0:4, :, at, :].reshape(256, COLUMNS),
            first,
        )

    def whole(slot):
        accumulate(
            lambda rows: normed[slot, :, :, rows].reshape(256, MB),
            lambda: grads[slot].reshape(256, COLUMNS),
        )

    up[2].wait_recv()
    up[3].wait_recv()
    down[0].wait_recv()
    down[1].wait_recv()
    swap[0].wait_recv()
    swap[1].wait_recv()
    near(0, first=True)

    f2_up[0].wait_recv()
    f2_down[0].wait_recv()
    f2_up[1].wait_recv()
    f4 = [grad_send(4, 1, 7, dh=1)]
    f2_down[1].wait_recv()
    f4 += [grad_send(4, 3, 7, dh=1)]

    theirs_up.wait_recv()
    n2 += [same(tokens_of(1, -1, slots=low), dy=1)]
    theirs_down.wait_recv()
    n2 += [same(tokens_of(1, 1, slots=high), dy=-1)]
    pair_low, pair_high = pair_of(-1), pair_of(1)
    swap += [same(pair_low, dc=1), same(pair_high, dc=1)]

    x2[0].wait_recv()
    f5 = [grad_send(5, 0, 7, dz=1)]
    x2[1].wait_recv()
    f5 += [grad_send(6, 2, 7, dz=-1)]

    swap[2].wait_recv()
    near(-1)
    swap[3].wait_recv()
    near(1)
    for copy in n2:
        copy.wait_recv()
    swap += [same(pair_of(2), dc=1)]
    swap[4].wait_recv()
    handed = load(normed.at[7], last_normed, 12)
    near(2)
    whole(4)
    for copy in f3:
        copy.wait_recv()
    whole(5)
    whole(6)
    handed.wait()
    for copy in f4 + f5:
        copy.wait_recv()
    for copy in started:
        copy.wait_send()


def finish_kernel(total, normed, grads, out_hbm, stage, sems):
    def store(m):
        return pltpu.make_async_copy(stage.at[m % 2], out_hbm.at[pl.ds(m * 256, 256)], sems.at[m % 2])

    steps = FEATURES // 256
    for m in range(steps):
        rows = slice(m * 256, (m + 1) * 256)
        part = lax.dot_general(
            normed[:, :, rows].reshape(256, 256), grads[...].reshape(256, COLUMNS),
            CONTRACT_FIRST, preferred_element_type=jnp.float32,
        )
        if m >= 2:
            store(m - 2).wait()
        stage[m % 2] = (total[rows, :] + part).astype(jnp.bfloat16)
        store(m).start()
    store(steps - 2).wait()
    store(steps - 1).wait()


def on_device(ckpt_values, ckpt_scales, norm_gain, pre_act, act_grad):
    any_space = pl.BlockSpec(memory_space=pl.ANY)
    vmem = pl.BlockSpec(memory_space=pltpu.VMEM)
    block = (REPLICAS, 2, HALF, COLUMNS)
    total, last_normed, last_grads = pl.pallas_call(
        gather_kernel,
        out_shape=(
            pltpu.VMEM((FEATURES, COLUMNS), jnp.float32),
            pltpu.VMEM(block[1:], jnp.bfloat16),
            pltpu.VMEM(block[1:], jnp.bfloat16),
        ),
        in_specs=[any_space] * 5,
        out_specs=(vmem, vmem, vmem),
        scratch_shapes=[
            pltpu.VMEM(block, jnp.bfloat16),
            pltpu.VMEM((REPLICAS - 1,) + block[1:], jnp.bfloat16),
            pltpu.VMEM((ROWS, WIDTH), jnp.bfloat16),
            pltpu.VMEM((ROWS, WIDTH // QB), jnp.bfloat16),
            pltpu.VMEM((1, WIDTH), jnp.float32),
            pltpu.VMEM((2 * HALF, COLUMNS), jnp.bfloat16),
            pltpu.VMEM((2 * HALF, COLUMNS), jnp.bfloat16),
            pltpu.VMEM((ROWS, WIDTH), jnp.float32),
            pltpu.VMEM((REPLICAS, ROWS, FEATURES), jnp.bfloat16),
            pltpu.SemaphoreType.DMA((COPIES,)),
            pltpu.SemaphoreType.DMA((COPIES,)),
            pltpu.SemaphoreType.DMA((13,)),
        ],
        compiler_params=pltpu.CompilerParams(
            collective_id=0, has_side_effects=True, vmem_limit_bytes=38 << 20
        ),
        name="gather_and_multiply",
    )(ckpt_values, ckpt_scales, norm_gain.reshape(1, WIDTH), pre_act, act_grad)
    return pl.pallas_call(
        finish_kernel,
        out_shape=jax.ShapeDtypeStruct((FEATURES, COLUMNS), jnp.bfloat16),
        in_specs=[vmem, vmem, vmem],
        out_specs=any_space,
        scratch_shapes=[pltpu.VMEM((2, 256, COLUMNS), jnp.bfloat16), pltpu.SemaphoreType.DMA((2,))],
        compiler_params=pltpu.CompilerParams(vmem_limit_bytes=8 << 20),
        name="add_last_replica",
    )(total, last_normed, last_grads)


def solution(mesh):
    in_specs = (
        P(("dp", "tensor"), None),
        P(("dp", "tensor"), None),
        P(),
        P("dp", "tensor"),
        P("dp", "tensor"),
    )
    return jax.shard_map(
        on_device, mesh=mesh, in_specs=in_specs, out_specs=P("dp", "tensor"), check_vma=False
    )
```

time: 407 us -> 100 us (0.25)
  blocking collectives: 112 us -> 0 us
  Pallas kernels: 0 us -> 99.9 us
  other arithmetic: 99.5 us -> 0 us
  local copies, waits for them, and re-layouts: 90.3 us -> 0 us
  waiting for transfers between devices: 59.3 us -> 0 us
  matrix products: 29.3 us -> 0 us
  between operations: 13.5 us -> 0.17 us
    all_to_all x1 -> x0, blocking collectives: 112 us -> none  [on_device(): lax.all_to_all(gathered[None], 'dp', split_axis=2, concat_axis=0, tiled=T...]
    pallas_call x0 -> x2, Pallas kernels: none -> 99.9 us  [the longest x1 91.7 us: on_device(): pl.pallas_call(gather_kernel, out_shape=(pltpu.VMEM((FEATURES, COLUMNS),...]
    unnamed x1 -> x0, other arithmetic: 95 us -> none
    all_gather x2 -> x0, waiting for transfers between devices: 59.3 us -> none  [the longest x1 59.3 us: on_device(): gathered = lax.all_gather(normed, 'tensor', axis=0, tiled=True)]
    broadcast_in_dim x1 -> x0, local copies, waits for them, and re-layouts: 38.5 us -> none  [on_device(): gathered[None]]
    unnamed x12 -> x0, local copies, waits for them, and re-layouts: 38.1 us -> none
    dot_general x1 -> x0, matrix products: 29.3 us -> none  [on_device(): lax.dot_general(features, lax.all_gather(pre_grad, 'dp', axis=0, tiled=Tr...]
    all_to_all x1 -> x0, local copies, waits for them, and re-layouts: 12.6 us -> none  [on_device(): lax.all_to_all(gathered[None], 'dp', split_axis=2, concat_axis=0, tiled=T...]
  transfers between devices with their start and end apart: 2 -> 0, of which waited for: 1 -> 0; matrix products, arithmetic and copies ran while one was open for 46% -> 0% of each run, Pallas kernels for 0% -> 0%
where the time goes in v1:
time: 100 us
  Pallas kernels  99.9 us (100%)
    pallas_call x1, Pallas kernels, on_device(): pl.pallas_call(gather_kernel, out_shape=(pltpu.VMEM((FEATURES, COLUMNS),...  91.7 us
    pallas_call x1, Pallas kernels, on_device(): pl.pallas_call(finish_kernel, out_shape=jax.ShapeDtypeStruct((FEATURES, C...  8.26 us

profile of v1, /device:TPU:1, one launch (start us, length us, event | category | flops | bytes accessed | tf_op | source)
XLA Modules:
  0.0 100.1 jit_solution(1147922404545220999)
XLA Ops:
  0.0 91.7 %gather_and_multiply.1 = (f32[2304,2304]{1,0:T(8,128)S(1)}, bf16[2,128,2304]{2,1,0:T(8,128)(2,1)S(1)}, bf16[2,128,2304]{2,1,0:T(8,128)(2,1)S(1)}) custom-call(bf16[16,18432]{1,0:T(8,128)(2,1)} %values_hbm.1, bf16[16,144]{1,0:T(8,128)(2,1)} %scales_hbm.1, f32[1,18432]{1,0:T(1,128)} %bitcast.1, bf16[256,2304]{1,0:T(8,128)(2,1)} %pre_hbm.1, ...), custom_call_target="tpu_custom_call" | custom-call | tf_op jit(solution)/shard_map/gather_and_multiply/pallas_call | solution.py:294
  91.7 8.3 %add_last_replica.1 = bf16[2304,2304]{1,0:T(8,128)(2,1)} custom-call(f32[2304,2304]{1,0:T(8,128)S(1)} %get-tuple-element.8.total, bf16[2,128,2304]{2,1,0:T(8,128)(2,1)S(1)} %get-tuple-element.9.normed, bf16[2,128,2304]{2,1,0:T(8,128)(2,1)S(1)} %get-tuple-element.10.grads), custom_call_target="tpu_custom_call" | custom-call | tf_op jit(solution)/shard_map/add_last_replica/pallas_call | solution.py:322

commit v2 on v1

v2 whole, which is shorter than its diff:
```python
import functools

import jax
import jax.numpy as jnp
from jax import lax
from jax.experimental import pallas as pl
from jax.experimental.pallas import tpu as pltpu
from jax.sharding import PartitionSpec as P

MESH = pl.DeviceIdType.MESH
QB = 128
REPLICAS = 8
GROUP = 16
ROWS = 16
FEATURES = 2304
COLUMNS = 2304
WIDTH = 18432
HALF = 128
CHUNK = 64
MB = 768

SLOT = {(0, 0): 0, (0, -1): 1, (0, 1): 2, (1, 0): 3, (0, 2): 4, (1, -1): 5, (1, 1): 6, (1, 2): 7}
EXCHANGED = (3, 5, 6, 7)
FAR = ((0, -1), (0, 1), (1, 0), (0, 2), (1, -1), (1, 1), (1, 2))
CONTRACT_FIRST = (((0,), (0,)), ((), ()))
COPIES = 80
SIDE = 1152
MOVED = 16


def gather_kernel(
    values_hbm, scales_hbm, gain_hbm, pre_hbm, act_hbm,
    left_done, right_total, last_normed, last_grads,
    left_total, normed, grads, values, scales, gain, pre, act, scaled, own, send_sems, recv_sems, local_sems,
):
    dp, tensor = lax.axis_index("dp"), lax.axis_index("tensor")
    h, z = dp // 4, dp % 4
    xl, y, core = tensor // 8, (tensor // 2) % 4, tensor % 2

    def peer(dh=0, dz=0, dx=0, dy=0, dc=0):
        return (
            (h + dh) % 2 * 4 + (z + dz + 4) % 4,
            (xl + dx) % 2 * 8 + (y + dy + 4) % 4 * 2 + (core + dc) % 2,
        )

    started = []

    def send(src, dst, device):
        at = len(started)
        copy = pltpu.make_async_remote_copy(
            src_ref=src, dst_ref=dst, send_sem=send_sems.at[at], recv_sem=recv_sems.at[at],
            device_id=device, device_id_type=MESH,
        )
        copy.start()
        started.append(copy)
        return copy

    def arrived(*copies):
        for copy in copies:
            copy.wait_recv()

    def load(src, dst, at):
        copy = pltpu.make_async_copy(src, dst, local_sems.at[at])
        copy.start()
        return copy

    def offset(c):
        return (c + y // 2) % 2 * CHUNK

    def load_chunk(c):
        rows = pl.ds(pl.multiple_of(c // 2 * HALF + offset(c), CHUNK), CHUNK)
        return load(pre_hbm.at[rows], pre.at[c], 2 * c), load(act_hbm.at[rows], act.at[c], 2 * c + 1)

    loads = {c: load_chunk(c) for c in (0, 2)}
    tokens = (load(values_hbm, values, 8), load(scales_hbm, scales, 9), load(gain_hbm, gain, 10))
    loads.update({c: load_chunk(c) for c in (1, 3)})

    friends = [peer(dh, dz, dx=dh) for dh, dz in FAR]
    friends += [peer(dh=1), peer(dx=1), peer(dy=1), peer(dy=-1), peer(dc=1)]
    barrier = pltpu.get_barrier_semaphore()
    for friend in friends:
        pl.semaphore_signal(barrier, inc=1, device_id=friend, device_id_type=MESH)

    def make_grad(c, first=0, count=CHUNK):
        rows = slice(first, first + count)
        product = act[c, rows].astype(jnp.float32) * 2.0 * jnp.maximum(pre[c, rows].astype(jnp.float32), 0.0)
        to = pl.ds(pl.multiple_of(offset(c) + first, 32), count)
        grads[0, c // 2, to] = product.astype(jnp.bfloat16)

    def chunk(slot, c, first, count, columns):
        ref = last_grads if slot == 7 else grads.at[slot]
        half = 1 - c // 2 if slot in EXCHANGED else c // 2
        return ref.at[half, pl.ds(pl.multiple_of(offset(c) + first, 16), count), columns]

    def pass_on(slot, c, to_slot, first=0, count=CHUNK, columns=slice(0, COLUMNS), **where):
        return send(chunk(slot, c, first, count, columns), chunk(to_slot, c, first, count, columns), peer(**where))

    def ready(c):
        for copy in loads[c]:
            copy.wait()

    ready(0)
    make_grad(0, 0, 32)
    pl.semaphore_wait(barrier, len(friends))
    up = {0: [pass_on(0, 0, 1, 0, 32, dz=1)]}
    over = {0: [pass_on(0, 0, 3, 0, 32, dh=1)]}
    ready(2)
    make_grad(2, 0, 32)
    down = {2: [pass_on(0, 2, 2, 0, 32, dz=-1)]}

    for copy in tokens:
        copy.wait()
    squares = jnp.zeros((ROWS, QB), jnp.float32)
    for b in range(WIDTH // QB):
        at = slice(b * QB, (b + 1) * QB)
        block = values[:, at].astype(jnp.float32) * scales[:, b : b + 1].astype(jnp.float32)
        scaled[:, at] = block
        squares = squares + block * block
    mean = jnp.sum(squares, axis=1, keepdims=True) * (1.0 / WIDTH)
    inverse = lax.rsqrt(mean + 1e-05)
    for d in range(REPLICAS):
        at = slice(d * FEATURES, (d + 1) * FEATURES)
        own[d] = (scaled[:, at] * inverse * gain[:, at]).astype(jnp.bfloat16)

    def place(dx=0, dy=0, slots=slice(0, 8)):
        at = pl.multiple_of((y + dy + 4) % 4 * 32 + core * 16, 16)
        return normed.at[slots, (xl + dx) % 2, pl.ds(at, ROWS)]

    def pair_of(dy):
        at = pl.multiple_of((y + dy + 4) % 4 * 32 + core * 16, 16)
        return normed.at[:, :, pl.ds(at, ROWS)]

    kept = load(own.at[dp], place().at[0], 11)
    spread = []
    for dh, dz in FAR:
        slot = SLOT[(dh, dz if dz == 2 else -dz)]
        to, place_in_group = peer(dh, dz, dx=dh)
        spread.append(send(own.at[to], place(dx=dh).at[slot], (to, place_in_group)))

    make_grad(0, 32, 32)
    up[0] += [pass_on(0, 0, 1, 32, 32, dz=1)]
    over[0] += [pass_on(0, 0, 3, 32, 32, dh=1)]
    make_grad(2, 32, 32)
    down[2] += [pass_on(0, 2, 2, 32, 32, dz=-1)]
    ready(1)
    make_grad(1)
    up[1] = [pass_on(0, 1, 1, dz=1)]
    ready(3)
    make_grad(3)
    down[3] = [pass_on(0, 3, 2, dz=-1)]
    up[2] = [pass_on(0, 2, 1, dz=1)]
    down[0] = [pass_on(0, 0, 2, dz=-1)]
    up[3] = [pass_on(0, 3, 1, dz=1)]
    down[1] = [pass_on(0, 1, 2, dz=-1)]

    low, high = slice(0, 4), slice(4, 8)

    def same(ref, **where):
        return send(ref, ref, peer(**where))

    kept.wait()
    arrived(*spread[:3])
    cross = [same(place(slots=low), dx=1)]
    mine_up, mine_down = [same(place(slots=low), dy=1)], [same(place(slots=low), dy=-1)]
    arrived(*spread[3:])
    cross += [same(place(slots=high), dx=1)]
    mine_up += [same(place(slots=high), dy=1)]
    mine_down += [same(place(slots=high), dy=-1)]
    swap = [same(place(), dc=1)]
    over[2] = [pass_on(0, 2, 3, dh=1)]
    over[1] = [pass_on(0, 1, 3, dh=1)]
    over[3] = [pass_on(0, 3, 3, dh=1)]

    arrived(*up[0])
    far = [pass_on(1, 0, 4, dz=1)]
    side_up = [pass_on(1, 0, 5, dh=1)]
    arrived(*down[2])
    far += [pass_on(2, 2, 4, dz=-1)]
    side_down = [pass_on(2, 2, 6, dh=1)]
    arrived(*over[0])
    side_down += [pass_on(3, 0, 6, dz=-1)]
    arrived(mine_up[0])
    mine_on = [same(place(dy=-1, slots=low), dy=1)]
    arrived(*up[1])
    far_up = pass_on(1, 1, 4, dz=1)
    side_up += [pass_on(1, 1, 5, 0, MOVED, dh=1)]
    arrived(*down[3])
    far_down = pass_on(2, 3, 4, dz=-1)
    side_down += [pass_on(2, 3, 6, 0, MOVED, dh=1)]
    arrived(cross[0])
    theirs_up, theirs_down = [same(place(dx=1, slots=low), dy=1)], [same(place(dx=1, slots=low), dy=-1)]
    arrived(mine_down[1])
    mine_on += [same(place(dy=1, slots=high), dy=-1)]
    arrived(cross[1])
    theirs_up += [same(place(dx=1, slots=high), dy=1)]
    theirs_down += [same(place(dx=1, slots=high), dy=-1)]
    swap += [same(place(dx=1), dc=1)]
    arrived(*over[2])
    side_up += [pass_on(3, 2, 5, dz=1)]

    def accumulate(left, right, first=False):
        def step(m, carry):
            out_rows = pl.ds(pl.multiple_of(m * MB, MB), MB)
            part = lax.dot_general(
                left(out_rows), right(), CONTRACT_FIRST, preferred_element_type=jnp.float32
            )
            if first:
                left_total[out_rows, :] = part[:, :SIDE]
                right_total[out_rows, :] = part[:, SIDE:]
            else:
                left_total[out_rows, :] += part[:, :SIDE]
                right_total[out_rows, :] += part[:, SIDE:]
            return carry

        lax.fori_loop(0, FEATURES // MB, step, 0)

    def near(dy, first=False):
        at = pl.ds(pl.multiple_of((y + dy + 4) % 4 * 32, 32), 32)
        accumulate(
            lambda rows: normed[0:4, :, at, rows].reshape(256, MB),
            lambda: grads[0:4, :, at, :].reshape(256, COLUMNS),
            first,
        )

    def whole(slot):
        accumulate(
            lambda rows: normed[slot, :, :, rows].reshape(256, MB),
            lambda: grads[slot].reshape(256, COLUMNS),
        )

    def beside(c):
        at = pl.ds(pl.multiple_of(offset(c), CHUNK), CHUNK)
        accumulate(
            lambda rows: normed[5:7, :, at, rows].reshape(256, MB),
            lambda: grads[5:7, :, at, :].reshape(256, COLUMNS),
        )

    arrived(*up[2], *down[0], swap[0], swap[1])
    near(0, first=True)

    arrived(theirs_up[0])
    theirs_on = [same(place(dx=1, dy=-1, slots=low), dy=1)]
    arrived(theirs_down[1])
    theirs_on += [same(place(dx=1, dy=1, slots=high), dy=-1)]
    arrived(*over[1])
    side_up += [pass_on(3, 1, 5, MOVED, CHUNK - MOVED, dz=1)]
    side_down += [pass_on(3, 1, 6, dz=-1)]
    arrived(mine_up[1], theirs_up[1])
    swap += [same(pair_of(-1), dc=1)]
    arrived(mine_down[0], theirs_down[0])
    swap += [same(pair_of(1), dc=1)]
    arrived(far_up)
    left, right = slice(0, SIDE), slice(SIDE, COLUMNS)
    arrived(*over[3])
    side_up += [pass_on(3, 3, 5, dz=1)]
    side_down += [pass_on(3, 3, 6, MOVED, CHUNK - MOVED, dz=-1)]

    arrived(*up[3], *down[1], swap[2])
    near(-1)
    arrived(*mine_on, *theirs_on)
    swap += [same(pair_of(2), dc=1)]
    arrived(far_down)
    last_left = [pass_on(4, 1, 7, columns=left, dh=1), pass_on(4, 3, 7, columns=left, dh=1)]
    last_right = [pass_on(4, 1, 7, columns=right, dh=1), pass_on(4, 3, 7, columns=right, dh=1)]
    arrived(swap[3])
    near(1)
    arrived(side_up[0])
    last_left += [pass_on(5, 0, 7, columns=left, dz=1)]
    last_right += [pass_on(5, 0, 7, columns=right, dz=1)]
    arrived(swap[4])
    handed = load(normed.at[7], last_normed, 12)
    near(2)
    arrived(side_down[0])
    last_left += [pass_on(6, 2, 7, columns=left, dz=-1)]
    last_right += [pass_on(6, 2, 7, columns=right, dz=-1)]
    arrived(*far)
    whole(4)
    arrived(side_up[2], side_down[1])
    beside(0)
    arrived(side_up[1], *side_up[3:], *side_down[2:])
    beside(1)
    arrived(*last_left)

    def finish(m, carry):
        rows = pl.ds(pl.multiple_of(m * MB, MB), MB)
        part = lax.dot_general(
            normed[7, :, :, rows].reshape(256, MB), last_grads[:, :, :SIDE].reshape(256, SIDE),
            CONTRACT_FIRST, preferred_element_type=jnp.float32,
        )
        left_done[rows, :] = (left_total[rows, :] + part).astype(jnp.bfloat16)
        return carry

    lax.fori_loop(0, FEATURES // MB, finish, 0)
    handed.wait()
    arrived(*last_right)
    for copy in started:
        copy.wait_send()


def finish_kernel(left_done, right_total, normed, grads, out_hbm, stage, sems):
    steps = FEATURES // MB
    left = pltpu.make_async_copy(left_done, out_hbm.at[:, pl.ds(0, SIDE)], sems.at[steps])
    left.start()
    stores = []
    for m in range(steps):
        rows = slice(m * MB, (m + 1) * MB)
        part = lax.dot_general(
            normed[:, :, rows].reshape(256, MB), grads[:, :, SIDE:].reshape(256, SIDE),
            CONTRACT_FIRST, preferred_element_type=jnp.float32,
        )
        stage[m] = (right_total[rows, :] + part).astype(jnp.bfloat16)
        stores.append(
            pltpu.make_async_copy(stage.at[m], out_hbm.at[pl.ds(m * MB, MB), pl.ds(SIDE, SIDE)], sems.at[m])
        )
        stores[m].start()
    left.wait()
    for store in stores:
        store.wait()


def on_device(ckpt_values, ckpt_scales, norm_gain, pre_act, act_grad):
    any_space = pl.BlockSpec(memory_space=pl.ANY)
    vmem = pl.BlockSpec(memory_space=pltpu.VMEM)
    block = (REPLICAS, 2, HALF, COLUMNS)
    parts = pl.pallas_call(
        gather_kernel,
        out_shape=(
            pltpu.VMEM((FEATURES, SIDE), jnp.bfloat16),
            pltpu.VMEM((FEATURES, SIDE), jnp.float32),
            pltpu.VMEM(block[1:], jnp.bfloat16),
            pltpu.VMEM(block[1:], jnp.bfloat16),
        ),
        in_specs=[any_space] * 5,
        out_specs=(vmem,) * 4,
        scratch_shapes=[
            pltpu.VMEM((FEATURES, SIDE), jnp.float32),
            pltpu.VMEM(block, jnp.bfloat16),
            pltpu.VMEM((REPLICAS - 1,) + block[1:], jnp.bfloat16),
            pltpu.VMEM((ROWS, WIDTH), jnp.bfloat16),
            pltpu.VMEM((ROWS, WIDTH // QB), jnp.bfloat16),
            pltpu.VMEM((1, WIDTH), jnp.float32),
            pltpu.VMEM((4, CHUNK, COLUMNS), jnp.bfloat16),
            pltpu.VMEM((4, CHUNK, COLUMNS), jnp.bfloat16),
            pltpu.VMEM((ROWS, WIDTH), jnp.float32),
            pltpu.VMEM((REPLICAS, ROWS, FEATURES), jnp.bfloat16),
            pltpu.SemaphoreType.DMA((COPIES,)),
            pltpu.SemaphoreType.DMA((COPIES,)),
            pltpu.SemaphoreType.DMA((13,)),
        ],
        compiler_params=pltpu.CompilerParams(
            collective_id=0, has_side_effects=True, vmem_limit_bytes=38 << 20
        ),
        name="gather_and_multiply",
    )(ckpt_values, ckpt_scales, norm_gain.reshape(1, WIDTH), pre_act, act_grad)
    return pl.pallas_call(
        finish_kernel,
        out_shape=jax.ShapeDtypeStruct((FEATURES, COLUMNS), jnp.bfloat16),
        in_specs=[vmem] * 4,
        out_specs=any_space,
        scratch_shapes=[pltpu.VMEM((3, MB, SIDE), jnp.bfloat16), pltpu.SemaphoreType.DMA((4,))],
        compiler_params=pltpu.CompilerParams(vmem_limit_bytes=8 << 20),
        name="add_last_replica",
    )(*parts)


def solution(mesh):
    in_specs = (
        P(("dp", "tensor"), None),
        P(("dp", "tensor"), None),
        P(),
        P("dp", "tensor"),
        P("dp", "tensor"),
    )
    return jax.shard_map(
        on_device, mesh=mesh, in_specs=in_specs, out_specs=P("dp", "tensor"), check_vma=False
    )
```

time: 100 us -> 84.8 us (0.85)
  Pallas kernels: 99.9 us -> 84.3 us
    pallas_call x1, Pallas kernels: 91.7 us -> 80.3 us  [on_device(): pl.pallas_call(gather_kernel, out_shape=(pltpu.VMEM((FEATURES, SIDE), jnp...]
    pallas_call x1, Pallas kernels: 8.26 us -> 4.07 us  [on_device(): pl.pallas_call(finish_kernel, out_shape=jax.ShapeDtypeStruct((FEATURES, C...]
where the time goes in v2:
time: 84.8 us; the launch traced here: 84.3 us
  Pallas kernels  84.3 us (99%)
    pallas_call x1, Pallas kernels, on_device(): pl.pallas_call(gather_kernel, out_shape=(pltpu.VMEM((FEATURES, SIDE), jnp...  80.3 us
    pallas_call x1, Pallas kernels, on_device(): pl.pallas_call(finish_kernel, out_shape=jax.ShapeDtypeStruct((FEATURES, C...  4.07 us

profile of v2, /device:TPU:1, one launch (start us, length us, event | category | flops | bytes accessed | tf_op | source)
XLA Modules:
  0.0 84.3 jit_solution(15114835139480582785)
XLA Ops:
  0.0 80.3 %gather_and_multiply.1 = (bf16[2304,1152]{1,0:T(8,128)(2,1)S(1)}, f32[2304,1152]{1,0:T(8,128)S(1)}, bf16[2,128,2304]{2,1,0:T(8,128)(2,1)S(1)}, bf16[2,128,2304]{2,1,0:T(8,128)(2,1)S(1)}) custom-call(bf16[16,18432]{1,0:T(8,128)(2,1)} %values_hbm.1, bf16[16,144]{1,0:T(8,128)(2,1)} %scales_hbm.1, f32[1,18432]{1,0:T(1,128)} %bitcast.1, ...), custom_call_target="tpu_custom_call" | custom-call | tf_op jit(solution)/shard_map/gather_and_multiply/pallas_call | solution.py:325
  80.3 4.1 %add_last_replica.1 = bf16[2304,2304]{1,0:T(8,128)(2,1)} custom-call(bf16[2304,1152]{1,0:T(8,128)(2,1)S(1)} %get-tuple-element.9.left_done, f32[2304,1152]{1,0:T(8,128)S(1)} %get-tuple-element.10.right_total, bf16[2,128,2304]{2,1,0:T(8,128)(2,1)S(1)} %get-tuple-element.11.normed, bf16[2,128,2304]{2,1,0:T(8,128)(2,1)S(1)} %get-tuple-element.12.grads), custom_call_target="tpu_custom_call" | custom-call | tf_op jit(solution)/shard_map/add_last_replica/pallas_call | solution.py:355

commit v3 on v2

--- a/solution.py
+++ b/solution.py
@@ -19,9 +19,9 @@
 CHUNK = 64
 MB = 768
 
-SLOT = {(0, 0): 0, (0, -1): 1, (0, 1): 2, (1, 0): 3, (0, 2): 4, (1, -1): 5, (1, 1): 6, (1, 2): 7}
-EXCHANGED = (3, 5, 6, 7)
-FAR = ((0, -1), (0, 1), (1, 0), (0, 2), (1, -1), (1, 1), (1, 2))
+SLOT = {(0, 0): 0, (0, -1): 1, (0, 1): 2, (0, 2): 3, (1, 0): 4, (1, -1): 5, (1, 1): 6, (1, 2): 7}
+EXCHANGED = (4, 5, 6, 7)
+FAR = ((0, -1), (0, 1), (0, 2), (1, 0), (1, -1), (1, 1), (1, 2))
 CONTRACT_FIRST = (((0,), (0,)), ((), ()))
 COPIES = 80
 SIDE = 1152
@@ -71,9 +71,8 @@
         rows = pl.ds(pl.multiple_of(c // 2 * HALF + offset(c), CHUNK), CHUNK)
         return load(pre_hbm.at[rows], pre.at[c], 2 * c), load(act_hbm.at[rows], act.at[c], 2 * c + 1)
 
-    loads = {c: load_chunk(c) for c in (0, 2)}
     tokens = (load(values_hbm, values, 8), load(scales_hbm, scales, 9), load(gain_hbm, gain, 10))
-    loads.update({c: load_chunk(c) for c in (1, 3)})
+    loads = {c: load_chunk(c) for c in (0, 2, 1, 3)}
 
     friends = [peer(dh, dz, dx=dh) for dh, dz in FAR]
     friends += [peer(dh=1), peer(dx=1), peer(dy=1), peer(dy=-1), peer(dc=1)]
@@ -81,11 +80,11 @@
     for friend in friends:
         pl.semaphore_signal(barrier, inc=1, device_id=friend, device_id_type=MESH)
 
-    def make_grad(c, first=0, count=CHUNK):
-        rows = slice(first, first + count)
-        product = act[c, rows].astype(jnp.float32) * 2.0 * jnp.maximum(pre[c, rows].astype(jnp.float32), 0.0)
-        to = pl.ds(pl.multiple_of(offset(c) + first, 32), count)
-        grads[0, c // 2, to] = product.astype(jnp.bfloat16)
+    def make_grad(c):
+        for copy in loads[c]:
+            copy.wait()
+        product = act[c].astype(jnp.float32) * 2.0 * jnp.maximum(pre[c].astype(jnp.float32), 0.0)
+        grads[0, c // 2, pl.ds(pl.multiple_of(offset(c), CHUNK), CHUNK)] = product.astype(jnp.bfloat16)
 
     def chunk(slot, c, first, count, columns):
         ref = last_grads if slot == 7 else grads.at[slot]
@@ -94,19 +93,6 @@
 
     def pass_on(slot, c, to_slot, first=0, count=CHUNK, columns=slice(0, COLUMNS), **where):
         return send(chunk(slot, c, first, count, columns), chunk(to_slot, c, first, count, columns), peer(**where))
-
-    def ready(c):
-        for copy in loads[c]:
-            copy.wait()
-
-    ready(0)
-    make_grad(0, 0, 32)
-    pl.semaphore_wait(barrier, len(friends))
-    up = {0: [pass_on(0, 0, 1, 0, 32, dz=1)]}
-    over = {0: [pass_on(0, 0, 3, 0, 32, dh=1)]}
-    ready(2)
-    make_grad(2, 0, 32)
-    down = {2: [pass_on(0, 2, 2, 0, 32, dz=-1)]}
 
     for copy in tokens:
         copy.wait()
@@ -122,6 +108,9 @@
         at = slice(d * FEATURES, (d + 1) * FEATURES)
         own[d] = (scaled[:, at] * inverse * gain[:, at]).astype(jnp.bfloat16)
 
+    make_grad(0)
+    pl.semaphore_wait(barrier, len(friends))
+
     def place(dx=0, dy=0, slots=slice(0, 8)):
         at = pl.multiple_of((y + dy + 4) % 4 * 32 + core * 16, 16)
         return normed.at[slots, (xl + dx) % 2, pl.ds(at, ROWS)]
@@ -132,20 +121,18 @@
 
     kept = load(own.at[dp], place().at[0], 11)
     spread = []
-    for dh, dz in FAR:
+    for dh, dz in FAR[4:] + FAR[:4]:
         slot = SLOT[(dh, dz if dz == 2 else -dz)]
         to, place_in_group = peer(dh, dz, dx=dh)
         spread.append(send(own.at[to], place(dx=dh).at[slot], (to, place_in_group)))
 
-    make_grad(0, 32, 32)
-    up[0] += [pass_on(0, 0, 1, 32, 32, dz=1)]
-    over[0] += [pass_on(0, 0, 3, 32, 32, dh=1)]
-    make_grad(2, 32, 32)
-    down[2] += [pass_on(0, 2, 2, 32, 32, dz=-1)]
-    ready(1)
+    up, down, over = {}, {}, {}
+    up[0] = [pass_on(0, 0, 1, dz=1)]
+    over[0] = [pass_on(0, 0, 4, dh=1)]
+    make_grad(2)
+    down[2] = [pass_on(0, 2, 2, dz=-1)]
     make_grad(1)
     up[1] = [pass_on(0, 1, 1, dz=1)]
-    ready(3)
     make_grad(3)
     down[3] = [pass_on(0, 3, 2, dz=-1)]
     up[2] = [pass_on(0, 2, 1, dz=1)]
@@ -159,44 +146,45 @@
         return send(ref, ref, peer(**where))
 
     kept.wait()
-    arrived(*spread[:3])
+    arrived(*spread[3:6])
     cross = [same(place(slots=low), dx=1)]
     mine_up, mine_down = [same(place(slots=low), dy=1)], [same(place(slots=low), dy=-1)]
-    arrived(*spread[3:])
+    arrived(*spread[:3], spread[6])
     cross += [same(place(slots=high), dx=1)]
     mine_up += [same(place(slots=high), dy=1)]
     mine_down += [same(place(slots=high), dy=-1)]
     swap = [same(place(), dc=1)]
-    over[2] = [pass_on(0, 2, 3, dh=1)]
-    over[1] = [pass_on(0, 1, 3, dh=1)]
-    over[3] = [pass_on(0, 3, 3, dh=1)]
-
+    over[2] = [pass_on(0, 2, 4, dh=1)]
+
+    far, side = {}, {}
     arrived(*up[0])
-    far = [pass_on(1, 0, 4, dz=1)]
-    side_up = [pass_on(1, 0, 5, dh=1)]
+    far[0] = pass_on(1, 0, 3, dz=1)
     arrived(*down[2])
-    far += [pass_on(2, 2, 4, dz=-1)]
-    side_down = [pass_on(2, 2, 6, dh=1)]
+    far[2] = pass_on(2, 2, 3, dz=-1)
     arrived(*over[0])
-    side_down += [pass_on(3, 0, 6, dz=-1)]
+    side["d0"] = pass_on(4, 0, 6, dz=-1)
+    arrived(cross[0])
+    theirs_up, theirs_down = [same(place(dx=1, slots=low), dy=1)], [same(place(dx=1, slots=low), dy=-1)]
     arrived(mine_up[0])
     mine_on = [same(place(dy=-1, slots=low), dy=1)]
     arrived(*up[1])
-    far_up = pass_on(1, 1, 4, dz=1)
-    side_up += [pass_on(1, 1, 5, 0, MOVED, dh=1)]
+    far[1] = pass_on(1, 1, 3, dz=1)
     arrived(*down[3])
-    far_down = pass_on(2, 3, 4, dz=-1)
-    side_down += [pass_on(2, 3, 6, 0, MOVED, dh=1)]
-    arrived(cross[0])
-    theirs_up, theirs_down = [same(place(dx=1, slots=low), dy=1)], [same(place(dx=1, slots=low), dy=-1)]
-    arrived(mine_down[1])
-    mine_on += [same(place(dy=1, slots=high), dy=-1)]
+    far[3] = pass_on(2, 3, 3, dz=-1)
     arrived(cross[1])
+    over[1] = [pass_on(0, 1, 4, dh=1)]
+    over[3] = [pass_on(0, 3, 4, dh=1)]
     theirs_up += [same(place(dx=1, slots=high), dy=1)]
     theirs_down += [same(place(dx=1, slots=high), dy=-1)]
     swap += [same(place(dx=1), dc=1)]
+    side["u0"] = pass_on(1, 0, 5, dh=1)
+    side["d2"] = pass_on(2, 2, 6, dh=1)
+    side["moved"] = pass_on(1, 1, 5, 0, MOVED, dh=1)
+    side["moved_down"] = pass_on(2, 3, 6, 0, MOVED, dh=1)
+    arrived(mine_down[1])
+    mine_on += [same(place(dy=1, slots=high), dy=-1)]
     arrived(*over[2])
-    side_up += [pass_on(3, 2, 5, dz=1)]
+    side["u2"] = pass_on(4, 2, 5, dz=1)
 
     def accumulate(left, right, first=False):
         def step(m, carry):
@@ -217,8 +205,12 @@
     def near(dy, first=False):
         at = pl.ds(pl.multiple_of((y + dy + 4) % 4 * 32, 32), 32)
         accumulate(
-            lambda rows: normed[0:4, :, at, rows].reshape(256, MB),
-            lambda: grads[0:4, :, at, :].reshape(256, COLUMNS),
+            lambda rows: jnp.concatenate(
+                [normed[0:3, :, at, rows].reshape(192, MB), normed[4, :, at, rows].reshape(64, MB)]
+            ),
+            lambda: jnp.concatenate(
+                [grads[0:3, :, at, :].reshape(192, COLUMNS), grads[4, :, at, :].reshape(64, COLUMNS)]
+            ),
             first,
         )
 
@@ -242,42 +234,43 @@
     theirs_on = [same(place(dx=1, dy=-1, slots=low), dy=1)]
     arrived(theirs_down[1])
     theirs_on += [same(place(dx=1, dy=1, slots=high), dy=-1)]
-    arrived(*over[1])
-    side_up += [pass_on(3, 1, 5, MOVED, CHUNK - MOVED, dz=1)]
-    side_down += [pass_on(3, 1, 6, dz=-1)]
     arrived(mine_up[1], theirs_up[1])
     swap += [same(pair_of(-1), dc=1)]
     arrived(mine_down[0], theirs_down[0])
     swap += [same(pair_of(1), dc=1)]
-    arrived(far_up)
-    left, right = slice(0, SIDE), slice(SIDE, COLUMNS)
+    arrived(*over[1])
+    side["u1"] = pass_on(4, 1, 5, MOVED, CHUNK - MOVED, dz=1)
+    side["d1"] = pass_on(4, 1, 6, dz=-1)
+    arrived(far[1])
     arrived(*over[3])
-    side_up += [pass_on(3, 3, 5, dz=1)]
-    side_down += [pass_on(3, 3, 6, MOVED, CHUNK - MOVED, dz=-1)]
+    side["u3"] = pass_on(4, 3, 5, dz=1)
+    side["d3"] = pass_on(4, 3, 6, MOVED, CHUNK - MOVED, dz=-1)
 
     arrived(*up[3], *down[1], swap[2])
     near(-1)
     arrived(*mine_on, *theirs_on)
     swap += [same(pair_of(2), dc=1)]
-    arrived(far_down)
-    last_left = [pass_on(4, 1, 7, columns=left, dh=1), pass_on(4, 3, 7, columns=left, dh=1)]
-    last_right = [pass_on(4, 1, 7, columns=right, dh=1), pass_on(4, 3, 7, columns=right, dh=1)]
     arrived(swap[3])
     near(1)
-    arrived(side_up[0])
-    last_left += [pass_on(5, 0, 7, columns=left, dz=1)]
-    last_right += [pass_on(5, 0, 7, columns=right, dz=1)]
+
+    left, right = slice(0, SIDE), slice(SIDE, COLUMNS)
+    arrived(far[3])
+    last_left = [pass_on(3, 1, 7, columns=left, dh=1), pass_on(3, 3, 7, columns=left, dh=1)]
+    last_right = [pass_on(3, 1, 7, columns=right, dh=1), pass_on(3, 3, 7, columns=right, dh=1)]
     arrived(swap[4])
     handed = load(normed.at[7], last_normed, 12)
     near(2)
-    arrived(side_down[0])
+    arrived(side["u0"])
+    last_left += [pass_on(5, 0, 7, columns=left, dz=1)]
+    last_right += [pass_on(5, 0, 7, columns=right, dz=1)]
+    arrived(side["d2"])
     last_left += [pass_on(6, 2, 7, columns=left, dz=-1)]
     last_right += [pass_on(6, 2, 7, columns=right, dz=-1)]
-    arrived(*far)
-    whole(4)
-    arrived(side_up[2], side_down[1])
+    arrived(far[0], far[2])
+    whole(3)
+    arrived(side["u2"], side["d0"])
     beside(0)
-    arrived(side_up[1], *side_up[3:], *side_down[2:])
+    arrived(side["u1"], side["d1"], side["u3"], side["d3"], side["moved"], side["moved_down"])
     beside(1)
     arrived(*last_left)
 

time: 84.8 us -> 82.6 us (0.974)
  Pallas kernels: 84.3 us -> 82.5 us
    pallas_call x1, Pallas kernels: 80.3 us -> 78.4 us  [on_device(): pl.pallas_call(gather_kernel, out_shape=(pltpu.VMEM((FEATURES, SIDE), jnp...]
where the time goes in v3:
time: 82.6 us; the launch traced here: 82.5 us
  Pallas kernels  82.5 us (100%)
    pallas_call x1, Pallas kernels, on_device(): pl.pallas_call(gather_kernel, out_shape=(pltpu.VMEM((FEATURES, SIDE), jnp...  78.4 us
    pallas_call x1, Pallas kernels, on_device(): pl.pallas_call(finish_kernel, out_shape=jax.ShapeDtypeStruct((FEATURES, C...  4.07 us

profile of v3, /device:TPU:1, one launch (start us, length us, event | category | flops | bytes accessed | tf_op | source)
XLA Modules:
  0.0 82.5 jit_solution(12103847008225845123)
XLA Ops:
  0.0 78.4 %gather_and_multiply.1 = (bf16[2304,1152]{1,0:T(8,128)(2,1)S(1)}, f32[2304,1152]{1,0:T(8,128)S(1)}, bf16[2,128,2304]{2,1,0:T(8,128)(2,1)S(1)}, bf16[2,128,2304]{2,1,0:T(8,128)(2,1)S(1)}) custom-call(bf16[16,18432]{1,0:T(8,128)(2,1)} %values_hbm.1, bf16[16,144]{1,0:T(8,128)(2,1)} %scales_hbm.1, f32[1,18432]{1,0:T(1,128)} %bitcast.1, ...), custom_call_target="tpu_custom_call" | custom-call | tf_op jit(solution)/shard_map/gather_and_multiply/pallas_call | solution.py:318
  78.4 4.1 %add_last_replica.1 = bf16[2304,2304]{1,0:T(8,128)(2,1)} custom-call(bf16[2304,1152]{1,0:T(8,128)(2,1)S(1)} %get-tuple-element.9.left_done, f32[2304,1152]{1,0:T(8,128)S(1)} %get-tuple-element.10.right_total, bf16[2,128,2304]{2,1,0:T(8,128)(2,1)S(1)} %get-tuple-element.11.normed, bf16[2,128,2304]{2,1,0:T(8,128)(2,1)S(1)} %get-tuple-element.12.grads), custom_call_target="tpu_custom_call" | custom-call | tf_op jit(solution)/shard_map/add_last_replica/pallas_call | solution.py:348

commit v4 on v3

--- a/solution.py
+++ b/solution.py
@@ -1,4 +1,4 @@
-import functools
+import math
 
 import jax
 import jax.numpy as jnp
@@ -23,7 +23,7 @@
 EXCHANGED = (4, 5, 6, 7)
 FAR = ((0, -1), (0, 1), (0, 2), (1, 0), (1, -1), (1, 1), (1, 2))
 CONTRACT_FIRST = (((0,), (0,)), ((), ()))
-COPIES = 80
+WAITS = 32
 SIDE = 1152
 MOVED = 16
 
@@ -43,21 +43,35 @@
             (xl + dx) % 2 * 8 + (y + dy + 4) % 4 * 2 + (core + dc) % 2,
         )
 
-    started = []
-
-    def send(src, dst, device):
-        at = len(started)
-        copy = pltpu.make_async_remote_copy(
-            src_ref=src, dst_ref=dst, send_sem=send_sems.at[at], recv_sem=recv_sems.at[at],
-            device_id=device, device_id_type=MESH,
-        )
-        copy.start()
-        started.append(copy)
-        return copy
-
-    def arrived(*copies):
-        for copy in copies:
-            copy.wait_recv()
+    arrivals, departures, sizes = {}, {}, {}
+
+    def units(ref):
+        return math.prod(ref.shape) // (ROWS * FEATURES)
+
+    def send(src, dst, device, key=None):
+        size = units(src)
+        sizes[size] = sizes.get(size, 0) + 1
+        key = ("copy", len(arrivals)) if key is None else key
+        group = (size, (sizes[size] - 1) // 8)
+        for table, name in ((arrivals, key), (departures, group)):
+            at, count, total = table.get(name, (len(table), 0, 0))
+            table[name] = (at, count + 1, total + size)
+        pltpu.make_async_remote_copy(
+            src_ref=src, dst_ref=dst, send_sem=send_sems.at[departures[group][0]],
+            recv_sem=recv_sems.at[arrivals[key][0]], device_id=device, device_id_type=MESH,
+        ).start()
+        return key
+
+    def take(semaphore, total):
+        amount = normed.at[0, 0, pl.ds(0, ROWS * total)] if total <= 8 else normed.at[pl.ds(0, total // 8), 0]
+        assert units(amount) == total
+        pltpu.make_async_copy(amount, amount, semaphore).wait()
+
+    def arrived(*keys):
+        for key in dict.fromkeys(keys):
+            at, count, total = arrivals[key]
+            assert keys.count(key) == count
+            take(recv_sems.at[at], total)
 
     def load(src, dst, at):
         copy = pltpu.make_async_copy(src, dst, local_sems.at[at])
@@ -69,9 +83,11 @@
 
     def load_chunk(c):
         rows = pl.ds(pl.multiple_of(c // 2 * HALF + offset(c), CHUNK), CHUNK)
-        return load(pre_hbm.at[rows], pre.at[c], 2 * c), load(act_hbm.at[rows], act.at[c], 2 * c + 1)
-
-    tokens = (load(values_hbm, values, 8), load(scales_hbm, scales, 9), load(gain_hbm, gain, 10))
+        load(pre_hbm.at[rows], pre.at[c], c)
+        load(act_hbm.at[rows], act.at[c], c)
+        return local_sems.at[c]
+
+    tokens = (load(values_hbm, values, 4), load(scales_hbm, scales, 7), load(gain_hbm, gain, 8))
     loads = {c: load_chunk(c) for c in (0, 2, 1, 3)}
 
     friends = [peer(dh, dz, dx=dh) for dh, dz in FAR]
@@ -81,8 +97,7 @@
         pl.semaphore_signal(barrier, inc=1, device_id=friend, device_id_type=MESH)
 
     def make_grad(c):
-        for copy in loads[c]:
-            copy.wait()
+        take(loads[c], 8)
         product = act[c].astype(jnp.float32) * 2.0 * jnp.maximum(pre[c].astype(jnp.float32), 0.0)
         grads[0, c // 2, pl.ds(pl.multiple_of(offset(c), CHUNK), CHUNK)] = product.astype(jnp.bfloat16)
 
@@ -91,8 +106,9 @@
         half = 1 - c // 2 if slot in EXCHANGED else c // 2
         return ref.at[half, pl.ds(pl.multiple_of(offset(c) + first, 16), count), columns]
 
-    def pass_on(slot, c, to_slot, first=0, count=CHUNK, columns=slice(0, COLUMNS), **where):
-        return send(chunk(slot, c, first, count, columns), chunk(to_slot, c, first, count, columns), peer(**where))
+    def pass_on(slot, c, to_slot, first=0, count=CHUNK, columns=slice(0, COLUMNS), key=None, **where):
+        there = chunk(to_slot, c, first, count, columns)
+        return send(chunk(slot, c, first, count, columns), there, peer(**where), key)
 
     for copy in tokens:
         copy.wait()
@@ -119,12 +135,12 @@
         at = pl.multiple_of((y + dy + 4) % 4 * 32 + core * 16, 16)
         return normed.at[:, :, pl.ds(at, ROWS)]
 
-    kept = load(own.at[dp], place().at[0], 11)
+    kept = load(own.at[dp], place().at[0], 5)
     spread = []
     for dh, dz in FAR[4:] + FAR[:4]:
         slot = SLOT[(dh, dz if dz == 2 else -dz)]
         to, place_in_group = peer(dh, dz, dx=dh)
-        spread.append(send(own.at[to], place(dx=dh).at[slot], (to, place_in_group)))
+        spread.append(send(own.at[to], place(dx=dh).at[slot], (to, place_in_group), ("slices", dh)))
 
     up, down, over = {}, {}, {}
     up[0] = [pass_on(0, 0, 1, dz=1)]
@@ -135,38 +151,39 @@
     up[1] = [pass_on(0, 1, 1, dz=1)]
     make_grad(3)
     down[3] = [pass_on(0, 3, 2, dz=-1)]
-    up[2] = [pass_on(0, 2, 1, dz=1)]
-    down[0] = [pass_on(0, 0, 2, dz=-1)]
-    up[3] = [pass_on(0, 3, 1, dz=1)]
-    down[1] = [pass_on(0, 1, 2, dz=-1)]
+    up[2] = [pass_on(0, 2, 1, dz=1, key="first")]
+    down[0] = [pass_on(0, 0, 2, dz=-1, key="first")]
+    up[3] = [pass_on(0, 3, 1, dz=1, key="second")]
+    down[1] = [pass_on(0, 1, 2, dz=-1, key="second")]
 
     low, high = slice(0, 4), slice(4, 8)
 
-    def same(ref, **where):
-        return send(ref, ref, peer(**where))
+    def same(ref, key=None, **where):
+        return send(ref, ref, peer(**where), key)
 
     kept.wait()
     arrived(*spread[3:6])
     cross = [same(place(slots=low), dx=1)]
-    mine_up, mine_down = [same(place(slots=low), dy=1)], [same(place(slots=low), dy=-1)]
+    mine_up, mine_down = [same(place(slots=low), dy=1)], [same(place(slots=low), dy=-1, key="above")]
     arrived(*spread[:3], spread[6])
     cross += [same(place(slots=high), dx=1)]
-    mine_up += [same(place(slots=high), dy=1)]
+    mine_up += [same(place(slots=high), dy=1, key="below")]
     mine_down += [same(place(slots=high), dy=-1)]
-    swap = [same(place(), dc=1)]
+    swap = [same(place(), dc=1, key="first")]
     over[2] = [pass_on(0, 2, 4, dh=1)]
 
     far, side = {}, {}
     arrived(*up[0])
-    far[0] = pass_on(1, 0, 3, dz=1)
+    far[0] = pass_on(1, 0, 3, dz=1, key="far")
     arrived(*down[2])
-    far[2] = pass_on(2, 2, 3, dz=-1)
+    far[2] = pass_on(2, 2, 3, dz=-1, key="far")
     arrived(*over[0])
-    side["d0"] = pass_on(4, 0, 6, dz=-1)
+    side["d0"] = pass_on(4, 0, 6, dz=-1, key="beside0")
     arrived(cross[0])
-    theirs_up, theirs_down = [same(place(dx=1, slots=low), dy=1)], [same(place(dx=1, slots=low), dy=-1)]
+    theirs_up = [same(place(dx=1, slots=low), dy=1)]
+    theirs_down = [same(place(dx=1, slots=low), dy=-1, key="above")]
     arrived(mine_up[0])
-    mine_on = [same(place(dy=-1, slots=low), dy=1)]
+    mine_on = [same(place(dy=-1, slots=low), dy=1, key="opposite")]
     arrived(*up[1])
     far[1] = pass_on(1, 1, 3, dz=1)
     arrived(*down[3])
@@ -174,17 +191,17 @@
     arrived(cross[1])
     over[1] = [pass_on(0, 1, 4, dh=1)]
     over[3] = [pass_on(0, 3, 4, dh=1)]
-    theirs_up += [same(place(dx=1, slots=high), dy=1)]
+    theirs_up += [same(place(dx=1, slots=high), dy=1, key="below")]
     theirs_down += [same(place(dx=1, slots=high), dy=-1)]
-    swap += [same(place(dx=1), dc=1)]
+    swap += [same(place(dx=1), dc=1, key="first")]
     side["u0"] = pass_on(1, 0, 5, dh=1)
     side["d2"] = pass_on(2, 2, 6, dh=1)
-    side["moved"] = pass_on(1, 1, 5, 0, MOVED, dh=1)
-    side["moved_down"] = pass_on(2, 3, 6, 0, MOVED, dh=1)
+    side["moved"] = pass_on(1, 1, 5, 0, MOVED, dh=1, key="beside1")
+    side["moved_down"] = pass_on(2, 3, 6, 0, MOVED, dh=1, key="beside1")
     arrived(mine_down[1])
-    mine_on += [same(place(dy=1, slots=high), dy=-1)]
+    mine_on += [same(place(dy=1, slots=high), dy=-1, key="opposite")]
     arrived(*over[2])
-    side["u2"] = pass_on(4, 2, 5, dz=1)
+    side["u2"] = pass_on(4, 2, 5, dz=1, key="beside0")
 
     def accumulate(left, right, first=False):
         def step(m, carry):
@@ -231,20 +248,20 @@
     near(0, first=True)
 
     arrived(theirs_up[0])
-    theirs_on = [same(place(dx=1, dy=-1, slots=low), dy=1)]
+    theirs_on = [same(place(dx=1, dy=-1, slots=low), dy=1, key="opposite")]
     arrived(theirs_down[1])
-    theirs_on += [same(place(dx=1, dy=1, slots=high), dy=-1)]
+    theirs_on += [same(place(dx=1, dy=1, slots=high), dy=-1, key="opposite")]
     arrived(mine_up[1], theirs_up[1])
-    swap += [same(pair_of(-1), dc=1)]
+    swap += [same(pair_of(-1), dc=1, key="second")]
     arrived(mine_down[0], theirs_down[0])
     swap += [same(pair_of(1), dc=1)]
     arrived(*over[1])
-    side["u1"] = pass_on(4, 1, 5, MOVED, CHUNK - MOVED, dz=1)
-    side["d1"] = pass_on(4, 1, 6, dz=-1)
+    side["u1"] = pass_on(4, 1, 5, MOVED, CHUNK - MOVED, dz=1, key="beside1")
+    side["d1"] = pass_on(4, 1, 6, dz=-1, key="beside1")
     arrived(far[1])
     arrived(*over[3])
-    side["u3"] = pass_on(4, 3, 5, dz=1)
-    side["d3"] = pass_on(4, 3, 6, MOVED, CHUNK - MOVED, dz=-1)
+    side["u3"] = pass_on(4, 3, 5, dz=1, key="beside1")
+    side["d3"] = pass_on(4, 3, 6, MOVED, CHUNK - MOVED, dz=-1, key="beside1")
 
     arrived(*up[3], *down[1], swap[2])
     near(-1)
@@ -255,17 +272,17 @@
 
     left, right = slice(0, SIDE), slice(SIDE, COLUMNS)
     arrived(far[3])
-    last_left = [pass_on(3, 1, 7, columns=left, dh=1), pass_on(3, 3, 7, columns=left, dh=1)]
-    last_right = [pass_on(3, 1, 7, columns=right, dh=1), pass_on(3, 3, 7, columns=right, dh=1)]
+    last_left = [pass_on(3, 1, 7, columns=left, dh=1, key="left"), pass_on(3, 3, 7, columns=left, dh=1, key="left")]
+    last_right = [pass_on(3, 1, 7, columns=right, dh=1, key="right"), pass_on(3, 3, 7, columns=right, dh=1, key="right")]
     arrived(swap[4])
-    handed = load(normed.at[7], last_normed, 12)
+    handed = load(normed.at[7], last_normed, 6)
     near(2)
     arrived(side["u0"])
-    last_left += [pass_on(5, 0, 7, columns=left, dz=1)]
-    last_right += [pass_on(5, 0, 7, columns=right, dz=1)]
+    last_left += [pass_on(5, 0, 7, columns=left, dz=1, key="left")]
+    last_right += [pass_on(5, 0, 7, columns=right, dz=1, key="right")]
     arrived(side["d2"])
-    last_left += [pass_on(6, 2, 7, columns=left, dz=-1)]
-    last_right += [pass_on(6, 2, 7, columns=right, dz=-1)]
+    last_left += [pass_on(6, 2, 7, columns=left, dz=-1, key="left")]
+    last_right += [pass_on(6, 2, 7, columns=right, dz=-1, key="right")]
     arrived(far[0], far[2])
     whole(3)
     arrived(side["u2"], side["d0"])
@@ -286,8 +303,8 @@
     lax.fori_loop(0, FEATURES // MB, finish, 0)
     handed.wait()
     arrived(*last_right)
-    for copy in started:
-        copy.wait_send()
+    for at, _, total in departures.values():
+        take(send_sems.at[at], total)
 
 
 def finish_kernel(left_done, right_total, normed, grads, out_hbm, stage, sems):
@@ -336,9 +353,9 @@
             pltpu.VMEM((4, CHUNK, COLUMNS), jnp.bfloat16),
             pltpu.VMEM((ROWS, WIDTH), jnp.float32),
             pltpu.VMEM((REPLICAS, ROWS, FEATURES), jnp.bfloat16),
-            pltpu.SemaphoreType.DMA((COPIES,)),
-            pltpu.SemaphoreType.DMA((COPIES,)),
-            pltpu.SemaphoreType.DMA((13,)),
+            pltpu.SemaphoreType.DMA((12,)),
+            pltpu.SemaphoreType.DMA((WAITS,)),
+            pltpu.SemaphoreType.DMA((9,)),
         ],
         compiler_params=pltpu.CompilerParams(
             collective_id=0, has_side_effects=True, vmem_limit_bytes=38 << 20

time: 82.6 us -> 81.4 us (0.985)
  Pallas kernels: 82.5 us -> 81.3 us
    pallas_call x1, Pallas kernels: 78.4 us -> 77.2 us  [on_device(): pl.pallas_call(gather_kernel, out_shape=(pltpu.VMEM((FEATURES, SIDE), jnp...]
where the time goes in v4:
time: 81.4 us; the launch traced here: 81.3 us
  Pallas kernels  81.3 us (100%)
    pallas_call x1, Pallas kernels, on_device(): pl.pallas_call(gather_kernel, out_shape=(pltpu.VMEM((FEATURES, SIDE), jnp...  77.2 us
    pallas_call x1, Pallas kernels, on_device(): pl.pallas_call(finish_kernel, out_shape=jax.ShapeDtypeStruct((FEATURES, C...  4.07 us

profile of v4, /device:TPU:1, one launch (start us, length us, event | category | flops | bytes accessed | tf_op | source)
XLA Modules:
  0.0 81.3 jit_solution(18268349848461435289)
XLA Ops:
  0.0 77.2 %gather_and_multiply.1 = (bf16[2304,1152]{1,0:T(8,128)(2,1)S(1)}, f32[2304,1152]{1,0:T(8,128)S(1)}, bf16[2,128,2304]{2,1,0:T(8,128)(2,1)S(1)}, bf16[2,128,2304]{2,1,0:T(8,128)(2,1)S(1)}) custom-call(bf16[16,18432]{1,0:T(8,128)(2,1)} %values_hbm.1, bf16[16,144]{1,0:T(8,128)(2,1)} %scales_hbm.1, f32[1,18432]{1,0:T(1,128)} %bitcast.1, ...), custom_call_target="tpu_custom_call" | custom-call | tf_op jit(solution)/shard_map/gather_and_multiply/pallas_call | solution.py:335
  77.2 4.1 %add_last_replica.1 = bf16[2304,2304]{1,0:T(8,128)(2,1)} custom-call(bf16[2304,1152]{1,0:T(8,128)(2,1)S(1)} %get-tuple-element.9.left_done, f32[2304,1152]{1,0:T(8,128)S(1)} %get-tuple-element.10.right_total, bf16[2,128,2304]{2,1,0:T(8,128)(2,1)S(1)} %get-tuple-element.11.normed, bf16[2,128,2304]{2,1,0:T(8,128)(2,1)S(1)} %get-tuple-element.12.grads), custom_call_target="tpu_custom_call" | custom-call | tf_op jit(solution)/shard_map/add_last_replica/pallas_call | solution.py:365

commit v5 on v4

--- a/solution.py
+++ b/solution.py
@@ -88,13 +88,13 @@
         return local_sems.at[c]
 
     tokens = (load(values_hbm, values, 4), load(scales_hbm, scales, 7), load(gain_hbm, gain, 8))
-    loads = {c: load_chunk(c) for c in (0, 2, 1, 3)}
 
     friends = [peer(dh, dz, dx=dh) for dh, dz in FAR]
     friends += [peer(dh=1), peer(dx=1), peer(dy=1), peer(dy=-1), peer(dc=1)]
     barrier = pltpu.get_barrier_semaphore()
     for friend in friends:
         pl.semaphore_signal(barrier, inc=1, device_id=friend, device_id_type=MESH)
+    loads = {c: load_chunk(c) for c in (0, 2, 1, 3)}
 
     def make_grad(c):
         take(loads[c], 8)
@@ -120,11 +120,11 @@
         squares = squares + block * block
     mean = jnp.sum(squares, axis=1, keepdims=True) * (1.0 / WIDTH)
     inverse = lax.rsqrt(mean + 1e-05)
-    for d in range(REPLICAS):
-        at = slice(d * FEATURES, (d + 1) * FEATURES)
-        own[d] = (scaled[:, at] * inverse * gain[:, at]).astype(jnp.bfloat16)
-
-    make_grad(0)
+
+    def make_slice(to):
+        at = pl.ds(pl.multiple_of(to * FEATURES, QB), FEATURES)
+        own[to] = (scaled[:, at] * inverse * gain[:, at]).astype(jnp.bfloat16)
+
     pl.semaphore_wait(barrier, len(friends))
 
     def place(dx=0, dy=0, slots=slice(0, 8)):
@@ -135,12 +135,16 @@
         at = pl.multiple_of((y + dy + 4) % 4 * 32 + core * 16, 16)
         return normed.at[:, :, pl.ds(at, ROWS)]
 
-    kept = load(own.at[dp], place().at[0], 5)
     spread = []
     for dh, dz in FAR[4:] + FAR[:4]:
         slot = SLOT[(dh, dz if dz == 2 else -dz)]
         to, place_in_group = peer(dh, dz, dx=dh)
+        make_slice(to)
         spread.append(send(own.at[to], place(dx=dh).at[slot], (to, place_in_group), ("slices", dh)))
+
+    make_grad(0)
+    make_slice(dp)
+    kept = load(own.at[dp], place().at[0], 5)
 
     up, down, over = {}, {}, {}
     up[0] = [pass_on(0, 0, 1, dz=1)]

time: 81.4 us -> 81.4 us (level)
  no operation moved by 1% of the time
where the time goes in v5:
time: 81.4 us; the launch traced here: 81.3 us
  Pallas kernels  81.3 us (100%)
    pallas_call x1, Pallas kernels, on_device(): pl.pallas_call(gather_kernel, out_shape=(pltpu.VMEM((FEATURES, SIDE), jnp...  77.2 us
    pallas_call x1, Pallas kernels, on_device(): pl.pallas_call(finish_kernel, out_shape=jax.ShapeDtypeStruct((FEATURES, C...  4.07 us

profile of v5, /device:TPU:1, one launch (start us, length us, event | category | flops | bytes accessed | tf_op | source)
XLA Modules:
  0.0 81.3 jit_solution(2971270591719142460)
XLA Ops:
  0.0 77.2 %gather_and_multiply.1 = (bf16[2304,1152]{1,0:T(8,128)(2,1)S(1)}, f32[2304,1152]{1,0:T(8,128)S(1)}, bf16[2,128,2304]{2,1,0:T(8,128)(2,1)S(1)}, bf16[2,128,2304]{2,1,0:T(8,128)(2,1)S(1)}) custom-call(bf16[16,18432]{1,0:T(8,128)(2,1)} %values_hbm.1, bf16[16,144]{1,0:T(8,128)(2,1)} %scales_hbm.1, f32[1,18432]{1,0:T(1,128)} %bitcast.1, ...), custom_call_target="tpu_custom_call" | custom-call | tf_op jit(solution)/shard_map/gather_and_multiply/pallas_call | solution.py:339
  77.2 4.1 %add_last_replica.1 = bf16[2304,2304]{1,0:T(8,128)(2,1)} custom-call(bf16[2304,1152]{1,0:T(8,128)(2,1)S(1)} %get-tuple-element.9.left_done, f32[2304,1152]{1,0:T(8,128)S(1)} %get-tuple-element.10.right_total, bf16[2,128,2304]{2,1,0:T(8,128)(2,1)S(1)} %get-tuple-element.11.normed, bf16[2,128,2304]{2,1,0:T(8,128)(2,1)S(1)} %get-tuple-element.12.grads), custom_call_target="tpu_custom_call" | custom-call | tf_op jit(solution)/shard_map/add_last_replica/pallas_call | solution.py:369

commit v6 on v5

--- a/solution.py
+++ b/solution.py
@@ -143,14 +143,14 @@
         spread.append(send(own.at[to], place(dx=dh).at[slot], (to, place_in_group), ("slices", dh)))
 
     make_grad(0)
-    make_slice(dp)
-    kept = load(own.at[dp], place().at[0], 5)
 
     up, down, over = {}, {}, {}
     up[0] = [pass_on(0, 0, 1, dz=1)]
     over[0] = [pass_on(0, 0, 4, dh=1)]
     make_grad(2)
     down[2] = [pass_on(0, 2, 2, dz=-1)]
+    make_slice(dp)
+    kept = load(own.at[dp], place().at[0], 5)
     make_grad(1)
     up[1] = [pass_on(0, 1, 1, dz=1)]
     make_grad(3)

time: 81.4 us -> 81.3 us (level)
  no operation moved by 1% of the time
where the time goes in v6:
time: 81.3 us; the launch traced here: 81.2 us
  Pallas kernels  81.2 us (100%)
    pallas_call x1, Pallas kernels, on_device(): pl.pallas_call(gather_kernel, out_shape=(pltpu.VMEM((FEATURES, SIDE), jnp...  77.1 us
    pallas_call x1, Pallas kernels, on_device(): pl.pallas_call(finish_kernel, out_shape=jax.ShapeDtypeStruct((FEATURES, C...  4.07 us

profile of v6, /device:TPU:1, one launch (start us, length us, event | category | flops | bytes accessed | tf_op | source)
XLA Modules:
  0.0 81.2 jit_solution(8399889067943664988)
XLA Ops:
  0.0 77.1 %gather_and_multiply.1 = (bf16[2304,1152]{1,0:T(8,128)(2,1)S(1)}, f32[2304,1152]{1,0:T(8,128)S(1)}, bf16[2,128,2304]{2,1,0:T(8,128)(2,1)S(1)}, bf16[2,128,2304]{2,1,0:T(8,128)(2,1)S(1)}) custom-call(bf16[16,18432]{1,0:T(8,128)(2,1)} %values_hbm.1, bf16[16,144]{1,0:T(8,128)(2,1)} %scales_hbm.1, f32[1,18432]{1,0:T(1,128)} %bitcast.1, ...), custom_call_target="tpu_custom_call" | custom-call | tf_op jit(solution)/shard_map/gather_and_multiply/pallas_call | solution.py:339
  77.1 4.1 %add_last_replica.1 = bf16[2304,2304]{1,0:T(8,128)(2,1)} custom-call(bf16[2304,1152]{1,0:T(8,128)(2,1)S(1)} %get-tuple-element.9.left_done, f32[2304,1152]{1,0:T(8,128)S(1)} %get-tuple-element.10.right_total, bf16[2,128,2304]{2,1,0:T(8,128)(2,1)S(1)} %get-tuple-element.11.normed, bf16[2,128,2304]{2,1,0:T(8,128)(2,1)S(1)} %get-tuple-element.12.grads), custom_call_target="tpu_custom_call" | custom-call | tf_op jit(solution)/shard_map/add_last_replica/pallas_call | solution.py:369
